TPU v7x, 32 devices: a whole 2x2x4 slice. The times are simulated.
32 devices in a mesh: expert: 4 (over z), tp: 2 (over x), dp: 4 (over y, core).
Axes of the slice: x: 2, y: 2, z: 4, core: 2. Of those that a mesh axis runs over, the one named last changes fastest.
Arguments:
- hidden: bfloat16 [128, 6144], P(('expert', 'tp', 'dp')), may hold values from -400 to 400
- norm_gain: float32 [6144], replicated, may hold values from 0.1 to 1.9
- expert_ids: int32 [128, 2], P(('expert', 'tp', 'dp')), may hold values from 0 to 3, all different within a row; in each aligned block of 4 rows (0 to 3, 4 to 7, ...) at most 2 rows name the same one
- router_logits: float32 [128, 2], P(('expert', 'tp', 'dp')), may hold values from -6 to 6
- w_gate: bfloat16 [4, 6144, 8192], P('expert', None, ('tp', 'dp')), may hold values from -0.078125 to 0.078125
- w_up: bfloat16 [4, 6144, 8192], P('expert', None, ('tp', 'dp')), may hold values from -0.078125 to 0.078125
- w_down: bfloat16 [4, 8192, 6144], P('expert', ('tp', 'dp')), may hold values from -0.0625 to 0.0625
Outputs:
- moe_out: bfloat16 [128, 6144], P(('expert', 'tp', 'dp'))
Inputs may be any that keep to these rules, and one draw needn't show every extreme that they name: `expert_ids`: each token names two different experts; the tokens of one device name one expert at most 2 times.
All inputs are finite; a program needn't handle non-finite values.
Results may differ from a plain program's by a relative error of at most 0.015.
Values may be sent and summed in bfloat16 or wider, within the bound.
A program may use at most 64 MiB of HBM per device.

v0:
```python
import jax
import jax.numpy as jnp
from jax import lax
from jax.sharding import PartitionSpec as P

MOST = 2


def body(hidden, norm_gain, expert_ids, router_logits, w_gate, w_up, w_down):
    width = hidden.shape[1]
    values = hidden.astype(jnp.float32)
    inverse = lax.rsqrt(jnp.mean(values * values, axis=1, keepdims=True) + 1e-05)
    normed = (values * inverse * norm_gain[None, :]).astype(jnp.bfloat16)
    groups = lax.axis_size("expert")
    assigned = expert_ids.reshape(-1)
    onehot = (assigned[:, None] == jnp.arange(groups, dtype=jnp.int32)[None, :]).astype(jnp.int32)
    earlier = jnp.cumsum(onehot, axis=0) - onehot
    position = jnp.sum(earlier * onehot, axis=1)
    chosen = assigned[None, None, :] == jnp.arange(groups, dtype=jnp.int32)[:, None, None]
    placed = position[None, None, :] == jnp.arange(MOST, dtype=jnp.int32)[None, :, None]
    selector = (chosen & placed).astype(jnp.bfloat16).reshape(groups * MOST, assigned.shape[0])
    repeated = jnp.repeat(normed, 2, axis=0)
    bucket = jnp.dot(selector, repeated, preferred_element_type=jnp.float32).astype(jnp.bfloat16)
    arrived = lax.all_to_all(
        bucket.reshape(groups, MOST, width), "expert", split_axis=0, concat_axis=0, tiled=True
    )
    arrived = arrived.reshape(groups * MOST, width)
    gate_mat = w_gate[0]
    up_mat = w_up[0]
    down_mat = w_down[0]
    block_rows = lax.all_gather(arrived, ("tp", "dp"), axis=0, tiled=True)
    gate_val = jnp.dot(block_rows, gate_mat, preferred_element_type=jnp.float32)
    up_val = jnp.dot(block_rows, up_mat, preferred_element_type=jnp.float32)
    activations = (jax.nn.silu(gate_val) * up_val).astype(jnp.bfloat16)
    summed = lax.psum_scatter(
        jnp.dot(activations, down_mat, preferred_element_type=jnp.float32).astype(jnp.bfloat16),
        ("tp", "dp"),
        scatter_dimension=0,
        tiled=True,
    )
    outgoing = summed.reshape(groups, MOST, width)
    returned = lax.all_to_all(outgoing, "expert", split_axis=0, concat_axis=0, tiled=True)
    picked = jnp.dot(
        selector.T, returned.reshape(groups * MOST, width), preferred_element_type=jnp.float32
    )
    picked = picked.reshape(hidden.shape[0], 2, width)
    first = jax.nn.sigmoid(router_logits[:, 0] - router_logits[:, 1])
    second = jax.nn.sigmoid(router_logits[:, 1] - router_logits[:, 0])
    route_weight = jnp.stack([first, second], axis=1)
    combined = jnp.sum(picked * route_weight[:, :, None], axis=1)
    return combined.astype(jnp.bfloat16)


def solution(mesh):
    placed = (
        P(("expert", "tp", "dp"), None),
        P(),
        P(("expert", "tp", "dp"), None),
        P(("expert", "tp", "dp"), None),
        P("expert", None, ("tp", "dp")),
        P("expert", None, ("tp", "dp")),
        P("expert", ("tp", "dp"), None),
    )
    return jax.shard_map(
        body, mesh=mesh, in_specs=placed, out_specs=P(("expert", "tp", "dp"), None), check_vma=False
    )
```

profile of v0, /device:TPU:0, one launch (start us, length us, event | category | flops | bytes accessed | tf_op | source)
XLA Modules:
  0.0 105.4 jit_solution(1328459947626938204)
XLA Ops:
  6.5 0.0 reduce-scatter.2.cloned.1.call-start
  6.5 0.8 copy.14
  7.3 0.1 eq.51
  7.4 0.2 reduce_window_sum.11
  7.6 1.0 fusion.24
  8.6 0.9 fusion.26
  9.5 0.1 broadcast_in_dim.2
  9.6 0.1 convolution_convert_fusion
  9.8 0.1 reshape.92
  9.9 12.0 %all_to_all.10 = bf16[4,2,6144]{2,1,0:T(2,128)(2,1)S(1)} all-to-all(bf16[4,2,6144]{2,1,0:T(2,128)(2,1)S(1)} %reshape.92), channel_id=1, replica_groups=mesh['expert'=4,'tp'=2,'dp'=4] {'expert'}, dimensions={0} | all-to-all | bytes 196608 | tf_op jit(solution)/shard_map/all_to_all | solution.py:24
  21.9 10.4 %all_gather.3 = bf16[64,6144]{1,0:T(8,128)(2,1)S(1)} all-gather(bf16[8,6144]{1,0:T(8,128)(2,1)S(1)} %reshape.93), channel_id=1, replica_groups=mesh['expert'=4,'tp'=2,'dp'=4] {'tp','dp'}, dimensions={0}, use_global_device_ids=true | all-gather | bytes 884736 | tf_op jit(solution)/shard_map/all_gather | solution.py:31
  32.3 6.9 %fusion.4 = f32[64,1024]{1,0:T(8,128)S(1)} fusion(bf16[64,6144]{1,0:T(8,128)(2,1)S(1)} %all_gather.3, bf16[1,6144,1024]{2,1,0:T(8,128)(2,1)} %param.11), kind=kOutput, calls=%fused_computation.4 | convolution fusion | flops 805306368 | bytes 13631488 | tf_op jit(solution)/shard_map/dot_general | solution.py:32
  39.2 0.0 copy-start
  39.2 13.5 %fusion.6 = bf16[64,6144]{1,0:T(8,128)(2,1)} fusion(bf16[1,1024,6144]{2,1,0:T(8,128)(2,1)} %param.13, bf16[64,6144]{1,0:T(8,128)(2,1)S(1)} %all_gather.3, bf16[1,6144,1024]{2,1,0:T(8,128)(2,1)} %param.12, f32[64,1024]{1,0:T(8,128)S(1)} %fusion.4), kind=kOutput, calls=%fused_computation.6 | convolution fusion | flops 1611399168 | bytes 27000832 | tf_op jit(solution)/shard_map/dot_general | solution.py:36
  52.7 0.0 reduce-scatter.2.cloned.1.call-update
  52.7 33.0 %reduce-scatter.2.cloned.1.call-done = bf16[8,6144]{1,0:T(8,128)(2,1)} async-done(((bf16[64,6144]{1,0:T(8,128)(2,1)}), bf16[8,6144]{1,0:T(8,128)(2,1)}) %reduce-scatter.2.cloned.1.call-update) | async-done | bytes 98320 | tf_op jit(solution)/shard_map/reduce_scatter | solution.py:35
  85.7 1.6 %reshape.94 = bf16[4,2,6144]{2,1,0:T(2,128)(2,1)} reshape(bf16[8,6144]{1,0:T(8,128)(2,1)} %reduce-scatter.2.cloned.1.call-done) | data formatting | bytes 196608 | tf_op jit(solution)/shard_map/reshape | solution.py:41
  87.3 4.6 %all-to-all-start.1 = ((bf16[4,2,6144]{2,1,0:T(2,128)(2,1)}), bf16[4,2,6144]{2,1,0:T(2,128)(2,1)S(1)}, u32[]{:S(2)}, u32[]{:S(2)}) async-start(bf16[4,2,6144]{2,1,0:T(2,128)(2,1)} %reshape.94), calls=%async_computation.2 | async-start | bytes 196608 | tf_op jit(solution)/shard_map/all_to_all | solution.py:42
  91.9 0.0 copy-done
  91.9 0.1 copy.15
  92.0 5.7 %all-to-all-done.1 = bf16[4,2,6144]{2,1,0:T(2,128)(2,1)S(1)} async-done(((bf16[4,2,6144]{2,1,0:T(2,128)(2,1)}), bf16[4,2,6144]{2,1,0:T(2,128)(2,1)S(1)}, u32[]{:S(2)}, u32[]{:S(2)}) %all-to-all-start.1) | async-done | bytes 98336 | tf_op jit(solution)/shard_map/all_to_all | solution.py:42
  97.8 0.8 fusion.15
  (13 shorter events, 0.2 us)
Async XLA Ops:
  6.5 79.2 %reduce-scatter.2.cloned.1.call-start = ((), (), s32[]{:S(2)}) async-start(), calls=%async_computation.3 | async-start | bytes 884736 | tf_op jit(solution)/shard_map/reduce_scatter | solution.py:35
  39.2 52.7 %copy-start = (f32[4,2]{0,1:T(2,128)S(1)}, f32[4,2]{0,1:T(2,128)}, u32[]{:S(2)}) copy-start(f32[4,2]{0,1:T(2,128)} %param.10) | copy-start | bytes 100
  87.3 10.4 %all-to-all-start.1 = ((bf16[4,2,6144]{2,1,0:T(2,128)(2,1)}), bf16[4,2,6144]{2,1,0:T(2,128)(2,1)S(1)}, u32[]{:S(2)}, u32[]{:S(2)}) async-start(bf16[4,2,6144]{2,1,0:T(2,128)(2,1)} %reshape.94), calls=%async_computation.2 | async-start | bytes 196608 | tf_op jit(solution)/shard_map/all_to_all | solution.py:42
Sparse Core Ops, SparseCore 0:
  52.9 32.8 reduce-scatter.1
where the time goes:
time: 106 us; the launch traced here: 105 us
  waiting for transfers between devices  38.7 us (37%)
  blocking collectives  22.4 us (21%)
  matrix products  21.4 us (20%)
  between operations  13.5 us (13%)
  starting transfers between devices  4.59 us (4%)
  local copies, waits for them, and re-layouts  2.83 us (3%)
  other arithmetic  2.13 us (2%)
    reduce_scatter x1, waiting for transfers between devices, body(): lax.psum_scatter(jnp.dot(activations, down_mat, preferred_element_type=jn...  33 us
    dot_general x1, matrix products, body(): jnp.dot(activations, down_mat, preferred_element_type=jnp.float32)  13.5 us
    all_to_all x1, blocking collectives, body(): lax.all_to_all(bucket.reshape(groups, MOST, width), 'expert', split_axis=...  12 us
    all_gather x1, blocking collectives, body(): block_rows = lax.all_gather(arrived, ('tp', 'dp'), axis=0, tiled=True)  10.4 us
    dot_general x1, matrix products, body(): gate_val = jnp.dot(block_rows, gate_mat, preferred_element_type=jnp.float32)  6.86 us
    all_to_all x1, waiting for transfers between devices, body(): lax.all_to_all(outgoing, 'expert', split_axis=0, concat_axis=0, tiled=True)  5.7 us
    all_to_all x1, starting transfers between devices, body(): lax.all_to_all(outgoing, 'expert', split_axis=0, concat_axis=0, tiled=True)  4.59 us
  transfers between devices with their start and end apart: 2, of which 2 were waited for; matrix products, arithmetic and copies ran while one was open for 0% of the time, Pallas kernels for 0%

commit v1 on v0

v1 whole, which is shorter than its diff:
```python
import functools

import jax
import jax.numpy as jnp
from jax import lax
from jax.experimental import pallas as pl
from jax.experimental.pallas import tpu as pltpu
from jax.sharding import PartitionSpec as P

MOST = 2
MESH = pl.DeviceIdType.MESH
F32 = jnp.float32
BF16 = jnp.bfloat16


def sigmoid(v):
    return 1.0 / (1.0 + jnp.exp(-v))


def kernel(
    experts, tps, dps, kchunks, ochunks,
    hid, gain, ids, logits, wg, wu, wd,
    out,
    wgv, wuv, wdv, zsend, zrecv, xbuf, gacc, uacc, act, psend, precv, own, rsend, rrecv, qsend, qrecv,
    wsem, dsem, zss, zrs, xss, xrs, fss, frs, pss, prs, rss, rrs, qss, qrs,
):
    tokens, width = hid.shape
    kc, oc = width // kchunks, width // ochunks
    halves = dps // 2
    group = tps * halves
    rows = experts * MOST
    me_e, me_t, me_d = lax.axis_index("expert"), lax.axis_index("tp"), lax.axis_index("dp")
    parity, half = me_d % 2, me_d // 2
    me_g = me_t * halves + half

    def z_dev(e):
        return {"expert": e, "tp": me_t, "dp": me_d}

    def g_dev(g):
        return {"expert": me_e, "tp": g // halves, "dp": (g % halves) * 2 + parity}

    partner = {"expert": me_e, "tp": me_t, "dp": half * 2 + 1 - parity}
    z_peers = [(me_e + k) % experts for k in range(1, experts)]
    g_peers = [(me_g + k) % group for k in range(1, group)]

    def remote(src, dst, ss, rs, dev):
        return pltpu.make_async_remote_copy(
            src_ref=src, dst_ref=dst, send_sem=ss, recv_sem=rs, device_id=dev, device_id_type=MESH
        )

    wcopies, dcopies = [], []
    for c in range(kchunks):
        pair = (
            pltpu.make_async_copy(wg.at[0, pl.ds(c * kc, kc), :], wgv.at[c], wsem.at[0, c]),
            pltpu.make_async_copy(wu.at[0, pl.ds(c * kc, kc), :], wuv.at[c], wsem.at[1, c]),
        )
        for copy in pair:
            copy.start()
        wcopies.append(pair)
    for j in range(ochunks):
        copy = pltpu.make_async_copy(wd.at[0, :, pl.ds(j * oc, oc)], wdv.at[j], dsem.at[j])
        copy.start()
        dcopies.append(copy)

    barrier = pltpu.get_barrier_semaphore()
    devices = [z_dev(e) for e in z_peers] + [g_dev(g) for g in g_peers] + [partner]
    for dev in devices:
        pl.semaphore_signal(barrier, inc=1, device_id=dev, device_id_type=MESH)

    values = hid[...].astype(F32)
    inverse = lax.rsqrt(jnp.mean(values * values, axis=1, keepdims=True) + 1e-05)
    normed = (values * inverse * gain[...]).astype(BF16).astype(F32)
    place = lax.broadcasted_iota(jnp.int32, (rows, 1), 0)
    expert_of, slot = place // MOST, place % MOST
    taken = jnp.zeros((rows, 1), jnp.int32)
    bucket = jnp.zeros((rows, width), F32)
    coefs = []
    for t in range(tokens):
        first = jnp.where(expert_of == ids[t, 0], 1, 0)
        names = first + jnp.where(expert_of == ids[t, 1], 1, 0)
        chosen = (names * jnp.where(taken == slot, 1, 0)).astype(F32)
        taken = taken + names
        bucket = bucket + chosen * normed[t : t + 1, :]
        gap = jnp.full((rows, 1), logits[t, 0] - logits[t, 1], F32)
        firstf = first.astype(F32)
        coefs.append(chosen * (firstf * sigmoid(gap) + (1.0 - firstf) * sigmoid(-gap)))
    for c in range(kchunks):
        for e in range(experts):
            zsend[c, e] = bucket[e * MOST : (e + 1) * MOST, c * kc : (c + 1) * kc].astype(BF16)

    pl.semaphore_wait(barrier, len(devices))

    waits = []

    def go(copy):
        copy.start()
        waits.append(copy)

    for c in range(kchunks):
        for k, e in enumerate(z_peers):
            go(remote(zsend.at[c, e], zrecv.at[c, me_e], zss.at[c, k], zrs.at[c, me_e], z_dev(e)))
    for c in range(kchunks):
        zrecv[c, me_e] = zsend[c, me_e]

    def spread(c):
        for k, e in enumerate(z_peers):
            remote(zsend.at[c, e], zrecv.at[c, e], zss.at[c, k], zrs.at[c, e], z_dev(e)).wait_recv()
        block = jnp.concatenate([zrecv[c, e].astype(F32) for e in range(experts)], axis=0)
        xbuf[c, 0, me_g] = block.astype(BF16)
        mine = xbuf.at[c, 0, me_g]
        for k, g in enumerate(g_peers):
            go(remote(mine, mine, xss.at[c, k], xrs.at[c, me_g], g_dev(g)))
        go(remote(mine, xbuf.at[c, 1, me_g], fss.at[c, 0], frs.at[c, me_g], partner))

    def forward(c):
        for k, g in enumerate(g_peers):
            here = xbuf.at[c, 0, g]
            remote(here, here, xss.at[c, k], xrs.at[c, g], g_dev(g)).wait_recv()
            go(remote(here, xbuf.at[c, 1, g], fss.at[c, k + 1], frs.at[c, g], partner))

    def enter(c):
        for g in range(group):
            there = xbuf.at[c, 1, g]
            remote(there, there, fss.at[c, 0], frs.at[c, g], partner).wait_recv()
        x = xbuf[c].astype(F32).reshape(2 * group * rows, kc).astype(BF16)
        for copy, w, acc in zip(wcopies[c], (wgv, wuv), (gacc, uacc)):
            copy.wait()
            term = jnp.dot(x, w[c], preferred_element_type=F32)
            if c == 0:
                acc[...] = term
            else:
                acc[...] += term

    for c in range(kchunks):
        spread(c)
    forward(0)
    for c in range(kchunks):
        if c + 1 < kchunks:
            forward(c + 1)
        enter(c)
    gate = gacc[...]
    act[...] = (gate * sigmoid(gate) * uacc[...]).astype(BF16)

    def down(j):
        dcopies[j].wait()
        part = jnp.dot(act[...], wdv[j], preferred_element_type=F32)
        part = part.reshape(2, group, rows, oc)
        psend[j] = part[1].astype(BF16)
        own[j] = part[0]
        go(remote(psend.at[j], precv.at[j], pss.at[j], prs.at[j], partner))

    def reduce(j):
        remote(psend.at[j], precv.at[j], pss.at[j], prs.at[j], partner).wait_recv()
        rsend[j] = (own[j] + precv[j].astype(F32)).astype(BF16)
        for k, g in enumerate(g_peers):
            go(remote(rsend.at[j, g], rrecv.at[j, me_g], rss.at[j, k], rrs.at[j, me_g], g_dev(g)))

    def home(j):
        total = rsend[j, me_g].astype(F32)
        for k, g in enumerate(g_peers):
            remote(rsend.at[j, g], rrecv.at[j, g], rss.at[j, k], rrs.at[j, g], g_dev(g)).wait_recv()
            total = total + rrecv[j, g].astype(F32)
        for e in range(experts):
            qsend[j, e] = total[e * MOST : (e + 1) * MOST, :].astype(BF16)
        for k, e in enumerate(z_peers):
            go(remote(qsend.at[j, e], qrecv.at[j, me_e], qss.at[j, k], qrs.at[j, me_e], z_dev(e)))
        qrecv[j, me_e] = qsend[j, me_e]

    def combine(j):
        for k, e in enumerate(z_peers):
            remote(qsend.at[j, e], qrecv.at[j, e], qss.at[j, k], qrs.at[j, e], z_dev(e)).wait_recv()
        back = jnp.concatenate([qrecv[j, e].astype(F32) for e in range(experts)], axis=0)
        result = [jnp.sum(back * coef, axis=0, keepdims=True) for coef in coefs]
        out[:, j * oc : (j + 1) * oc] = jnp.concatenate(result, axis=0).astype(BF16)

    stages = (down, reduce, home, combine)
    lags = (0, 1, 3, 5)
    for step in range(ochunks + lags[-1]):
        for stage, lag in zip(stages, lags):
            if 0 <= step - lag < ochunks:
                stage(step - lag)

    for copy in waits:
        copy.wait_send()


def body(hidden, norm_gain, expert_ids, router_logits, w_gate, w_up, w_down):
    experts, tps, dps = lax.axis_size("expert"), lax.axis_size("tp"), lax.axis_size("dp")
    tokens, width = hidden.shape
    inner = w_gate.shape[2]
    kchunks, ochunks = 3, 4
    kc, oc = width // kchunks, width // ochunks
    group = tps * (dps // 2)
    rows = experts * MOST
    many = 2 * group * rows
    dma = pltpu.SemaphoreType.DMA
    vmem = pl.BlockSpec(memory_space=pltpu.VMEM)
    smem = pl.BlockSpec(memory_space=pltpu.SMEM)
    hbm = pl.BlockSpec(memory_space=pl.ANY)
    return pl.pallas_call(
        functools.partial(kernel, experts, tps, dps, kchunks, ochunks),
        out_shape=jax.ShapeDtypeStruct((tokens, width), BF16),
        in_specs=[vmem, vmem, smem, smem, hbm, hbm, hbm],
        out_specs=vmem,
        scratch_shapes=[
            pltpu.VMEM((kchunks, kc, inner), BF16),
            pltpu.VMEM((kchunks, kc, inner), BF16),
            pltpu.VMEM((ochunks, inner, oc), BF16),
            pltpu.VMEM((kchunks, experts, MOST, kc), BF16),
            pltpu.VMEM((kchunks, experts, MOST, kc), BF16),
            pltpu.VMEM((kchunks, 2, group, rows, kc), BF16),
            pltpu.VMEM((many, inner), F32),
            pltpu.VMEM((many, inner), F32),
            pltpu.VMEM((many, inner), BF16),
            pltpu.VMEM((ochunks, group, rows, oc), BF16),
            pltpu.VMEM((ochunks, group, rows, oc), BF16),
            pltpu.VMEM((ochunks, group, rows, oc), F32),
            pltpu.VMEM((ochunks, group, rows, oc), BF16),
            pltpu.VMEM((ochunks, group, rows, oc), BF16),
            pltpu.VMEM((ochunks, experts, MOST, oc), BF16),
            pltpu.VMEM((ochunks, experts, MOST, oc), BF16),
            dma((2, kchunks)),
            dma((ochunks,)),
            dma((kchunks, experts)),
            dma((kchunks, experts)),
            dma((kchunks, group)),
            dma((kchunks, group)),
            dma((kchunks, group)),
            dma((kchunks, group)),
            dma((ochunks,)),
            dma((ochunks,)),
            dma((ochunks, group)),
            dma((ochunks, group)),
            dma((ochunks, experts)),
            dma((ochunks, experts)),
        ],
        compiler_params=pltpu.CompilerParams(
            collective_id=0, has_side_effects=True, vmem_limit_bytes=60 * 1024 * 1024
        ),
        cost_estimate=pl.CostEstimate(
            flops=6 * many * width * inner, bytes_accessed=6 * width * inner, transcendentals=many * inner
        ),
        name="expert_layer",
    )(hidden, norm_gain[None, :], expert_ids, router_logits, w_gate, w_up, w_down)


def solution(mesh):
    placed = (
        P(("expert", "tp", "dp"), None),
        P(),
        P(("expert", "tp", "dp"), None),
        P(("expert", "tp", "dp"), None),
        P("expert", None, ("tp", "dp")),
        P("expert", None, ("tp", "dp")),
        P("expert", ("tp", "dp"), None),
    )
    return jax.shard_map(
        body, mesh=mesh, in_specs=placed, out_specs=P(("expert", "tp", "dp"), None), check_vma=False
    )
```

time: 106 us -> 39 us (0.37)
  waiting for transfers between devices: 38.7 us -> 0 us
  Pallas kernels: 0 us -> 34.6 us
  blocking collectives: 22.4 us -> 0 us
  matrix products: 21.4 us -> 0 us
  between operations: 13.5 us -> 0.01 us
  starting transfers between devices: 4.59 us -> 0 us
  other arithmetic: 2.13 us -> 0 us
  local copies, waits for them, and re-layouts: 2.83 us -> 4.1 us
    pallas_call x0 -> x1, Pallas kernels: none -> 34.6 us  [body(): pl.pallas_call(functools.partial(kernel, experts, tps, dps, kchunks, ochu...]
    reduce_scatter x1 -> x0, waiting for transfers between devices: 33 us -> none  [body(): lax.psum_scatter(jnp.dot(activations, down_mat, preferred_element_type=jn...]
    dot_general x4 -> x0, matrix products: 21.4 us -> none  [the longest x1 13.5 us: body(): jnp.dot(activations, down_mat, preferred_element_type=jnp.float32)]
    all_to_all x1 -> x0, blocking collectives: 12 us -> none  [body(): lax.all_to_all(bucket.reshape(groups, MOST, width), 'expert', split_axis=...]
    all_gather x1 -> x0, blocking collectives: 10.4 us -> none  [body(): block_rows = lax.all_gather(arrived, ('tp', 'dp'), axis=0, tiled=True)]
    all_to_all x1 -> x0, waiting for transfers between devices: 5.7 us -> none  [body(): lax.all_to_all(outgoing, 'expert', split_axis=0, concat_axis=0, tiled=True)]
    all_to_all x1 -> x0, starting transfers between devices: 4.59 us -> none  [body(): lax.all_to_all(outgoing, 'expert', split_axis=0, concat_axis=0, tiled=True)]
    unnamed x3, local copies, waits for them, and re-layouts: 0.77 us -> 4.1 us
  transfers between devices with their start and end apart: 2 -> 0, of which waited for: 2 -> 0; matrix products, arithmetic and copies ran while one was open for 0% -> 0% of each run, Pallas kernels for 0% -> 0%
where the time goes in v1:
time: 39 us; the launch traced here: 38.7 us
  Pallas kernels  34.6 us (89%)
  local copies, waits for them, and re-layouts  4.1 us (11%)
    pallas_call x1, Pallas kernels, body(): pl.pallas_call(functools.partial(kernel, experts, tps, dps, kchunks, ochu...  34.6 us
    unnamed x3, local copies, waits for them, and re-layouts  4.1 us

profile of v1, /device:TPU:0, one launch (start us, length us, event | category | flops | bytes accessed | tf_op | source)
XLA Modules:
  0.0 38.7 jit_solution(1666028357567802217)
XLA Ops:
  0.0 1.3 %copy.8.ids = s32[4,2]{1,0:T(4,128)} copy(s32[4,2]{0,1:T(2,128)} %param.9) | data formatting | bytes 64 | tf_op args[2]
  1.3 1.3 %copy.9.logits = f32[4,2]{1,0:T(4,128)} copy(f32[4,2]{0,1:T(2,128)} %param.10) | data formatting | bytes 64 | tf_op args[3]
  2.7 34.6 %expert_layer.1 = bf16[4,6144]{1,0:T(4,128)(2,1)} custom-call(bf16[4,6144]{1,0:T(4,128)(2,1)} %hid.1, f32[1,6144]{1,0:T(1,128)} %bitcast.1, s32[4,2]{1,0:T(4,128)} %copy.8.ids, f32[4,2]{1,0:T(4,128)} %copy.9.logits, bf16[1,6144,1024]{2,1,0:T(8,128)(2,1)} %wg.1, bf16[1,6144,1024]{2,1,0:T(8,128)(2,1)} %wu.1, bf16[1,1024,6144]{2,1,0:T(8,128)(2,1)} %wd.1), custom_call_target="tpu_custom_call" | custom-call | flops 2415919104 | bytes 37748736 | tf_op jit(solution)/shard_map/expert_layer/pallas_call | solution.py:200
  37.3 1.4 %copy.11 = bf16[4,6144]{1,0:T(4,128)(2,1)} copy(bf16[4,6144]{1,0:T(4,128)(2,1)} %expert_layer.1) | data formatting | bytes 98304

commit v2 on v1

--- a/solution.py
+++ b/solution.py
@@ -19,12 +19,13 @@
 
 def kernel(
     experts, tps, dps, kchunks, ochunks,
-    hid, gain, ids, logits, wg, wu, wd,
-    out,
-    wgv, wuv, wdv, zsend, zrecv, xbuf, gacc, uacc, act, psend, precv, own, rsend, rrecv, qsend, qrecv,
-    wsem, dsem, zss, zrs, xss, xrs, fss, frs, pss, prs, rss, rrs, qss, qrs,
+    hid_hbm, gain_hbm, ids_hbm, logits_hbm, wg, wu, wd,
+    back, coef_hbm,
+    hid, gain, ids, logits, coef,
+    wgv, wuv, wdv, zsend, zrecv, xbuf, gacc, uacc, act, psend, precv, own, rsend, rrecv, qsend,
+    isem, wsem, dsem, zss, zrs, xss, xrs, fss, frs, pss, prs, rss, rrs, qss, qrs,
 ):
-    tokens, width = hid.shape
+    tokens, width = hid_hbm.shape
     kc, oc = width // kchunks, width // ochunks
     halves = dps // 2
     group = tps * halves
@@ -48,24 +49,39 @@
             src_ref=src, dst_ref=dst, send_sem=ss, recv_sem=rs, device_id=dev, device_id_type=MESH
         )
 
-    wcopies, dcopies = [], []
-    for c in range(kchunks):
-        pair = (
-            pltpu.make_async_copy(wg.at[0, pl.ds(c * kc, kc), :], wgv.at[c], wsem.at[0, c]),
-            pltpu.make_async_copy(wu.at[0, pl.ds(c * kc, kc), :], wuv.at[c], wsem.at[1, c]),
-        )
-        for copy in pair:
-            copy.start()
-        wcopies.append(pair)
-    for j in range(ochunks):
-        copy = pltpu.make_async_copy(wd.at[0, :, pl.ds(j * oc, oc)], wdv.at[j], dsem.at[j])
-        copy.start()
-        dcopies.append(copy)
-
     barrier = pltpu.get_barrier_semaphore()
     devices = [z_dev(e) for e in z_peers] + [g_dev(g) for g in g_peers] + [partner]
     for dev in devices:
         pl.semaphore_signal(barrier, inc=1, device_id=dev, device_id_type=MESH)
+
+    small = [
+        pltpu.make_async_copy(src, dst, isem.at[i])
+        for i, (src, dst) in enumerate(
+            [(hid_hbm, hid), (gain_hbm, gain), (ids_hbm, ids), (logits_hbm, logits)]
+        )
+    ]
+    for copy in small:
+        copy.start()
+
+    wcopies = [
+        (
+            pltpu.make_async_copy(wg.at[0, pl.ds(c * kc, kc), :], wgv.at[c], wsem.at[0, c]),
+            pltpu.make_async_copy(wu.at[0, pl.ds(c * kc, kc), :], wuv.at[c], wsem.at[1, c]),
+        )
+        for c in range(kchunks)
+    ]
+    dcopies = [
+        pltpu.make_async_copy(wd.at[0, :, pl.ds(j * oc, oc)], wdv.at[j], dsem.at[j])
+        for j in range(ochunks)
+    ]
+
+    def fetch(c):
+        for copy in wcopies[c]:
+            copy.start()
+
+    fetch(0)
+    for copy in small:
+        copy.wait()
 
     values = hid[...].astype(F32)
     inverse = lax.rsqrt(jnp.mean(values * values, axis=1, keepdims=True) + 1e-05)
@@ -74,16 +90,17 @@
     expert_of, slot = place // MOST, place % MOST
     taken = jnp.zeros((rows, 1), jnp.int32)
     bucket = jnp.zeros((rows, width), F32)
-    coefs = []
     for t in range(tokens):
-        first = jnp.where(expert_of == ids[t, 0], 1, 0)
-        names = first + jnp.where(expert_of == ids[t, 1], 1, 0)
+        first = jnp.where(expert_of == ids[0, t], 1, 0)
+        names = first + jnp.where(expert_of == ids[1, t], 1, 0)
         chosen = (names * jnp.where(taken == slot, 1, 0)).astype(F32)
         taken = taken + names
         bucket = bucket + chosen * normed[t : t + 1, :]
-        gap = jnp.full((rows, 1), logits[t, 0] - logits[t, 1], F32)
+        gap = jnp.full((rows, 1), logits[0, t] - logits[1, t], F32)
         firstf = first.astype(F32)
-        coefs.append(chosen * (firstf * sigmoid(gap) + (1.0 - firstf) * sigmoid(-gap)))
+        coef[:, t : t + 1] = chosen * (firstf * sigmoid(gap) + (1.0 - firstf) * sigmoid(-gap))
+    coef_copy = pltpu.make_async_copy(coef, coef_hbm, isem.at[4])
+    coef_copy.start()
     for c in range(kchunks):
         for e in range(experts):
             zsend[c, e] = bucket[e * MOST : (e + 1) * MOST, c * kc : (c + 1) * kc].astype(BF16)
@@ -99,6 +116,7 @@
     for c in range(kchunks):
         for k, e in enumerate(z_peers):
             go(remote(zsend.at[c, e], zrecv.at[c, me_e], zss.at[c, k], zrs.at[c, me_e], z_dev(e)))
+    fetch(1)
     for c in range(kchunks):
         zrecv[c, me_e] = zsend[c, me_e]
 
@@ -131,9 +149,15 @@
             else:
                 acc[...] += term
 
-    for c in range(kchunks):
+    spread(0)
+    for c in range(2, kchunks):
+        fetch(c)
+    for c in range(1, kchunks):
         spread(c)
+    dcopies[0].start()
     forward(0)
+    for copy in dcopies[1:]:
+        copy.start()
     for c in range(kchunks):
         if c + 1 < kchunks:
             forward(c + 1)
@@ -163,23 +187,27 @@
         for e in range(experts):
             qsend[j, e] = total[e * MOST : (e + 1) * MOST, :].astype(BF16)
         for k, e in enumerate(z_peers):
-            go(remote(qsend.at[j, e], qrecv.at[j, me_e], qss.at[j, k], qrs.at[j, me_e], z_dev(e)))
-        qrecv[j, me_e] = qsend[j, me_e]
-
-    def combine(j):
-        for k, e in enumerate(z_peers):
-            remote(qsend.at[j, e], qrecv.at[j, e], qss.at[j, k], qrs.at[j, e], z_dev(e)).wait_recv()
-        back = jnp.concatenate([qrecv[j, e].astype(F32) for e in range(experts)], axis=0)
-        result = [jnp.sum(back * coef, axis=0, keepdims=True) for coef in coefs]
-        out[:, j * oc : (j + 1) * oc] = jnp.concatenate(result, axis=0).astype(BF16)
-
-    stages = (down, reduce, home, combine)
-    lags = (0, 1, 3, 5)
+            go(remote(qsend.at[j, e], cols(me_e, j), qss.at[j, k], qrs.at[j, me_e], z_dev(e)))
+        kept.append(pltpu.make_async_copy(qsend.at[j, me_e], cols(me_e, j), qrs.at[j, me_e]))
+        kept[-1].start()
+
+    kept = []
+
+    def cols(e, j):
+        return back.at[e, :, pl.ds(j * oc, oc)]
+
+    stages = (down, reduce, home)
+    lags = (0, 1, 3)
     for step in range(ochunks + lags[-1]):
         for stage, lag in zip(stages, lags):
             if 0 <= step - lag < ochunks:
                 stage(step - lag)
 
+    for j in range(ochunks):
+        for k, e in enumerate(z_peers):
+            remote(qsend.at[j, e], cols(e, j), qss.at[j, k], qrs.at[j, e], z_dev(e)).wait_recv()
+        kept[j].wait()
+    coef_copy.wait()
     for copy in waits:
         copy.wait_send()
 
@@ -194,15 +222,21 @@
     rows = experts * MOST
     many = 2 * group * rows
     dma = pltpu.SemaphoreType.DMA
-    vmem = pl.BlockSpec(memory_space=pltpu.VMEM)
-    smem = pl.BlockSpec(memory_space=pltpu.SMEM)
     hbm = pl.BlockSpec(memory_space=pl.ANY)
-    return pl.pallas_call(
+    back, coef = pl.pallas_call(
         functools.partial(kernel, experts, tps, dps, kchunks, ochunks),
-        out_shape=jax.ShapeDtypeStruct((tokens, width), BF16),
-        in_specs=[vmem, vmem, smem, smem, hbm, hbm, hbm],
-        out_specs=vmem,
+        out_shape=[
+            jax.ShapeDtypeStruct((experts, MOST, width), BF16),
+            jax.ShapeDtypeStruct((rows, tokens), F32),
+        ],
+        in_specs=[hbm] * 7,
+        out_specs=[hbm] * 2,
         scratch_shapes=[
+            pltpu.VMEM((tokens, width), BF16),
+            pltpu.VMEM((1, width), F32),
+            pltpu.SMEM((2, tokens), jnp.int32),
+            pltpu.SMEM((2, tokens), F32),
+            pltpu.VMEM((rows, tokens), F32),
             pltpu.VMEM((kchunks, kc, inner), BF16),
             pltpu.VMEM((kchunks, kc, inner), BF16),
             pltpu.VMEM((ochunks, inner, oc), BF16),
@@ -218,7 +252,7 @@
             pltpu.VMEM((ochunks, group, rows, oc), BF16),
             pltpu.VMEM((ochunks, group, rows, oc), BF16),
             pltpu.VMEM((ochunks, experts, MOST, oc), BF16),
-            pltpu.VMEM((ochunks, experts, MOST, oc), BF16),
+            dma((5,)),
             dma((2, kchunks)),
             dma((ochunks,)),
             dma((kchunks, experts)),
@@ -235,13 +269,16 @@
             dma((ochunks, experts)),
         ],
         compiler_params=pltpu.CompilerParams(
-            collective_id=0, has_side_effects=True, vmem_limit_bytes=60 * 1024 * 1024
+            collective_id=0, has_side_effects=True, vmem_limit_bytes=62 * 1024 * 1024
         ),
         cost_estimate=pl.CostEstimate(
             flops=6 * many * width * inner, bytes_accessed=6 * width * inner, transcendentals=many * inner
         ),
         name="expert_layer",
-    )(hidden, norm_gain[None, :], expert_ids, router_logits, w_gate, w_up, w_down)
+    )(hidden, norm_gain[None, :], expert_ids.T, router_logits.T, w_gate, w_up, w_down)
+    weight = coef.reshape(experts, MOST, tokens)
+    combined = jnp.sum(back.astype(F32)[:, :, None, :] * weight[:, :, :, None], axis=(0, 1))
+    return combined.astype(BF16)
 
 
 def solution(mesh):

time: 39 us -> 35.9 us (0.921)
  local copies, waits for them, and re-layouts: 4.1 us -> 0 us
  other arithmetic: 0 us -> 2.52 us
  Pallas kernels: 34.6 us -> 33.2 us
    unnamed x3 -> x0, local copies, waits for them, and re-layouts: 4.1 us -> none
    reduce_sum x0 -> x1, other arithmetic: none -> 1.56 us  [body(): jnp.sum(back.astype(F32)[:, :, None, :] * weight[:, :, :, None], axis=(0,...]
    pallas_call x1, Pallas kernels: 34.6 us -> 33.2 us  [body(): pl.pallas_call(functools.partial(kernel, experts, tps, dps, kchunks, ochu...]
    convert_element_type x0 -> x1, other arithmetic: none -> 0.96 us  [body(): back.astype(F32)[:, :, None, :] * weight[:, :, :, None]]
where the time goes in v2:
time: 35.9 us; the launch traced here: 35.7 us
  Pallas kernels  33.2 us (92%)
  other arithmetic  2.52 us (7%)
    pallas_call x1, Pallas kernels, body(): pl.pallas_call(functools.partial(kernel, experts, tps, dps, kchunks, ochu...  33.2 us
    reduce_sum x1, other arithmetic, body(): jnp.sum(back.astype(F32)[:, :, None, :] * weight[:, :, :, None], axis=(0,...  1.56 us
    convert_element_type x1, other arithmetic, body(): back.astype(F32)[:, :, None, :] * weight[:, :, :, None]  0.96 us

profile of v2, /device:TPU:0, one launch (start us, length us, event | category | flops | bytes accessed | tf_op | source)
XLA Modules:
  0.0 35.7 jit_solution(15086880457154361994)
XLA Ops:
  0.0 33.2 %expert_layer.1 = (bf16[4,2,6144]{2,1,0:T(2,128)(2,1)}, f32[8,4]{1,0:T(8,128)}) custom-call(bf16[4,6144]{1,0:T(4,128)(2,1)} %hid_hbm.1, f32[1,6144]{1,0:T(1,128)} %bitcast.4, s32[2,4]{1,0:T(2,128)} %bitcast.6, f32[2,4]{1,0:T(2,128)} %bitcast.7, bf16[1,6144,1024]{2,1,0:T(8,128)(2,1)} %wg.1, bf16[1,6144,1024]{2,1,0:T(8,128)(2,1)} %wu.1, bf16[1,1024,6144]{2,1,0:T(8,128)(2,1)} %wd.1), custom_call_target="tpu_custom_call" | custom-call | flops 2415919104 | bytes 37748736 | tf_op jit(solution)/shard_map/expert_layer/pallas_call | solution.py:226
  33.2 1.0 %convert_element_type.6 = f32[4,2,6144]{2,1,0:T(2,128)S(1)} convert(bf16[4,2,6144]{2,1,0:T(2,128)(2,1)} %get-tuple-element.7) | non-fusion elementwise | flops 49152 | bytes 294912 | tf_op jit(solution)/shard_map/convert_element_type | solution.py:280
  34.1 1.6 %multiply_reduce_fusion = bf16[4,6144]{1,0:T(4,128)(2,1)} fusion(f32[4,2,4]{2,1,0:T(2,128)} %bitcast.5, f32[4,2,6144]{2,1,0:T(2,128)S(1)} %convert_element_type.6), kind=kLoop, calls=%fused_computation | loop fusion | flops 368640 | bytes 245888 | tf_op jit(solution)/shard_map/reduce_sum | solution.py:280

commit v3 on v2

--- a/solution.py
+++ b/solution.py
@@ -85,27 +85,17 @@
 
     values = hid[...].astype(F32)
     inverse = lax.rsqrt(jnp.mean(values * values, axis=1, keepdims=True) + 1e-05)
-    normed = (values * inverse * gain[...]).astype(BF16).astype(F32)
     place = lax.broadcasted_iota(jnp.int32, (rows, 1), 0)
     expert_of, slot = place // MOST, place % MOST
     taken = jnp.zeros((rows, 1), jnp.int32)
-    bucket = jnp.zeros((rows, width), F32)
+    picks, firsts = [], []
     for t in range(tokens):
         first = jnp.where(expert_of == ids[0, t], 1, 0)
         names = first + jnp.where(expert_of == ids[1, t], 1, 0)
         chosen = (names * jnp.where(taken == slot, 1, 0)).astype(F32)
         taken = taken + names
-        bucket = bucket + chosen * normed[t : t + 1, :]
-        gap = jnp.full((rows, 1), logits[0, t] - logits[1, t], F32)
-        firstf = first.astype(F32)
-        coef[:, t : t + 1] = chosen * (firstf * sigmoid(gap) + (1.0 - firstf) * sigmoid(-gap))
-    coef_copy = pltpu.make_async_copy(coef, coef_hbm, isem.at[4])
-    coef_copy.start()
-    for c in range(kchunks):
-        for e in range(experts):
-            zsend[c, e] = bucket[e * MOST : (e + 1) * MOST, c * kc : (c + 1) * kc].astype(BF16)
-
-    pl.semaphore_wait(barrier, len(devices))
+        picks.append(chosen)
+        firsts.append(first.astype(F32))
 
     waits = []
 
@@ -113,12 +103,30 @@
         copy.start()
         waits.append(copy)
 
+    def settle():
+        for copy in waits:
+            copy.wait_send()
+        waits.clear()
+
+    pl.semaphore_wait(barrier, len(devices))
     for c in range(kchunks):
+        part = slice(c * kc, (c + 1) * kc)
+        normed = (values[:, part] * inverse * gain[:, part]).astype(BF16).astype(F32)
+        bucket = sum(pick * normed[t : t + 1, :] for t, pick in enumerate(picks))
+        for e in range(experts):
+            zsend[c, e] = bucket[e * MOST : (e + 1) * MOST, :].astype(BF16)
         for k, e in enumerate(z_peers):
             go(remote(zsend.at[c, e], zrecv.at[c, me_e], zss.at[c, k], zrs.at[c, me_e], z_dev(e)))
     fetch(1)
     for c in range(kchunks):
         zrecv[c, me_e] = zsend[c, me_e]
+
+    def weigh():
+        for t, (pick, first) in enumerate(zip(picks, firsts)):
+            gap = jnp.full((rows, 1), logits[0, t] - logits[1, t], F32)
+            coef[:, t : t + 1] = pick * (first * sigmoid(gap) + (1.0 - first) * sigmoid(-gap))
+
+    coef_copy = pltpu.make_async_copy(coef, coef_hbm, isem.at[4])
 
     def spread(c):
         for k, e in enumerate(z_peers):
@@ -152,6 +160,8 @@
     spread(0)
     for c in range(2, kchunks):
         fetch(c)
+    weigh()
+    coef_copy.start()
     for c in range(1, kchunks):
         spread(c)
     dcopies[0].start()
@@ -199,17 +209,35 @@
     stages = (down, reduce, home)
     lags = (0, 1, 3)
     for step in range(ochunks + lags[-1]):
+        if step == ochunks:
+            settle()
         for stage, lag in zip(stages, lags):
             if 0 <= step - lag < ochunks:
                 stage(step - lag)
 
+    coef_copy.wait()
+    settle()
     for j in range(ochunks):
+        kept[j].wait()
         for k, e in enumerate(z_peers):
             remote(qsend.at[j, e], cols(e, j), qss.at[j, k], qrs.at[j, e], z_dev(e)).wait_recv()
-        kept[j].wait()
-    coef_copy.wait()
-    for copy in waits:
-        copy.wait_send()
+
+
+def weighted_sum(back_hbm, coef_hbm, out, back, coef, sem):
+    copies = [
+        pltpu.make_async_copy(back_hbm, back, sem.at[0]),
+        pltpu.make_async_copy(coef_hbm, coef, sem.at[1]),
+    ]
+    for copy in copies:
+        copy.start()
+    for copy in copies:
+        copy.wait()
+    experts = back.shape[0]
+    rows = jnp.concatenate([back[e].astype(F32) for e in range(experts)], axis=0)
+    sums = [
+        jnp.sum(rows * coef[:, t : t + 1], axis=0, keepdims=True) for t in range(out.shape[0])
+    ]
+    out[...] = jnp.concatenate(sums, axis=0).astype(BF16)
 
 
 def body(hidden, norm_gain, expert_ids, router_logits, w_gate, w_up, w_down):
@@ -276,9 +304,19 @@
         ),
         name="expert_layer",
     )(hidden, norm_gain[None, :], expert_ids.T, router_logits.T, w_gate, w_up, w_down)
-    weight = coef.reshape(experts, MOST, tokens)
-    combined = jnp.sum(back.astype(F32)[:, :, None, :] * weight[:, :, :, None], axis=(0, 1))
-    return combined.astype(BF16)
+    return pl.pallas_call(
+        weighted_sum,
+        out_shape=jax.ShapeDtypeStruct((tokens, width), BF16),
+        in_specs=[hbm] * 2,
+        out_specs=pl.BlockSpec(memory_space=pltpu.VMEM),
+        scratch_shapes=[
+            pltpu.VMEM(back.shape, BF16),
+            pltpu.VMEM(coef.shape, F32),
+            dma((2,)),
+        ],
+        compiler_params=pltpu.CompilerParams(vmem_limit_bytes=62 * 1024 * 1024),
+        name="weighted_sum",
+    )(back, coef)
 
 
 def solution(mesh):

time: 35.9 us -> 36.5 us (1.017)
  Pallas kernels: 33.2 us -> 36.4 us
  other arithmetic: 2.52 us -> 0 us
    pallas_call x0 -> x1, Pallas kernels: none -> 1.82 us  [body(): pl.pallas_call(weighted_sum, out_shape=jax.ShapeDtypeStruct((tokens, widt...]
    reduce_sum x1 -> x0, other arithmetic: 1.56 us -> none  [body(): jnp.sum(back.astype(F32)[:, :, None, :] * weight[:, :, :, None], axis=(0,...]
    pallas_call x1, Pallas kernels: 33.2 us -> 34.6 us  [body(): pl.pallas_call(functools.partial(kernel, experts, tps, dps, kchunks, ochu...]
    convert_element_type x1 -> x0, other arithmetic: 0.96 us -> none  [body(): back.astype(F32)[:, :, None, :] * weight[:, :, :, None]]
where the time goes in v3:
time: 36.5 us; the launch traced here: 36.4 us
  Pallas kernels  36.4 us (100%)
    pallas_call x1, Pallas kernels, body(): pl.pallas_call(functools.partial(kernel, experts, tps, dps, kchunks, ochu...  34.6 us
    pallas_call x1, Pallas kernels, body(): pl.pallas_call(weighted_sum, out_shape=jax.ShapeDtypeStruct((tokens, widt...  1.82 us

profile of v3, /device:TPU:0, one launch (start us, length us, event | category | flops | bytes accessed | tf_op | source)
XLA Modules:
  0.0 36.4 jit_solution(1016501276964101159)
XLA Ops:
  0.0 34.6 %expert_layer.1 = (bf16[4,2,6144]{2,1,0:T(2,128)(2,1)}, f32[8,4]{1,0:T(8,128)}) custom-call(bf16[4,6144]{1,0:T(4,128)(2,1)} %hid_hbm.1, f32[1,6144]{1,0:T(1,128)} %bitcast.3, s32[2,4]{1,0:T(2,128)} %bitcast.4, f32[2,4]{1,0:T(2,128)} %bitcast.5, bf16[1,6144,1024]{2,1,0:T(8,128)(2,1)} %wg.1, bf16[1,6144,1024]{2,1,0:T(8,128)(2,1)} %wu.1, bf16[1,1024,6144]{2,1,0:T(8,128)(2,1)} %wd.1), custom_call_target="tpu_custom_call" | custom-call | flops 2415919104 | bytes 37748736 | tf_op jit(solution)/shard_map/expert_layer/pallas_call | solution.py:254
  34.6 1.8 %weighted_sum.1 = bf16[4,6144]{1,0:T(4,128)(2,1)} custom-call(bf16[4,2,6144]{2,1,0:T(2,128)(2,1)} %get-tuple-element.7.back_hbm, f32[8,4]{1,0:T(8,128)} %get-tuple-element.8.coef_hbm), custom_call_target="tpu_custom_call" | custom-call | tf_op jit(solution)/shard_map/weighted_sum/pallas_call | solution.py:307

commit v4 on v3

--- a/solution.py
+++ b/solution.py
@@ -79,7 +79,10 @@
         for copy in wcopies[c]:
             copy.start()
 
-    fetch(0)
+    for c in range(kchunks):
+        fetch(c)
+    for copy in dcopies:
+        copy.start()
     for copy in small:
         copy.wait()
 
@@ -108,16 +111,16 @@
             copy.wait_send()
         waits.clear()
 
-    pl.semaphore_wait(barrier, len(devices))
     for c in range(kchunks):
         part = slice(c * kc, (c + 1) * kc)
         normed = (values[:, part] * inverse * gain[:, part]).astype(BF16).astype(F32)
         bucket = sum(pick * normed[t : t + 1, :] for t, pick in enumerate(picks))
         for e in range(experts):
             zsend[c, e] = bucket[e * MOST : (e + 1) * MOST, :].astype(BF16)
+    pl.semaphore_wait(barrier, len(devices))
+    for c in range(kchunks):
         for k, e in enumerate(z_peers):
             go(remote(zsend.at[c, e], zrecv.at[c, me_e], zss.at[c, k], zrs.at[c, me_e], z_dev(e)))
-    fetch(1)
     for c in range(kchunks):
         zrecv[c, me_e] = zsend[c, me_e]
 
@@ -157,17 +160,9 @@
             else:
                 acc[...] += term
 
-    spread(0)
-    for c in range(2, kchunks):
-        fetch(c)
-    weigh()
-    coef_copy.start()
-    for c in range(1, kchunks):
+    for c in range(kchunks):
         spread(c)
-    dcopies[0].start()
     forward(0)
-    for copy in dcopies[1:]:
-        copy.start()
     for c in range(kchunks):
         if c + 1 < kchunks:
             forward(c + 1)
@@ -209,14 +204,14 @@
     stages = (down, reduce, home)
     lags = (0, 1, 3)
     for step in range(ochunks + lags[-1]):
-        if step == ochunks:
-            settle()
         for stage, lag in zip(stages, lags):
             if 0 <= step - lag < ochunks:
                 stage(step - lag)
 
+    weigh()
+    coef_copy.start()
+    settle()
     coef_copy.wait()
-    settle()
     for j in range(ochunks):
         kept[j].wait()
         for k, e in enumerate(z_peers):
@@ -244,7 +239,7 @@
     experts, tps, dps = lax.axis_size("expert"), lax.axis_size("tp"), lax.axis_size("dp")
     tokens, width = hidden.shape
     inner = w_gate.shape[2]
-    kchunks, ochunks = 3, 4
+    kchunks, ochunks = 3, 6
     kc, oc = width // kchunks, width // ochunks
     group = tps * (dps // 2)
     rows = experts * MOST

time: 36.5 us -> 42 us (1.15)
  Pallas kernels: 36.4 us -> 41.9 us
    pallas_call x1, Pallas kernels: 34.6 us -> 40.1 us  [body(): pl.pallas_call(functools.partial(kernel, experts, tps, dps, kchunks, ochu...]
where the time goes in v4:
time: 42 us; the launch traced here: 41.9 us
  Pallas kernels  41.9 us (100%)
    pallas_call x1, Pallas kernels, body(): pl.pallas_call(functools.partial(kernel, experts, tps, dps, kchunks, ochu...  40.1 us
    pallas_call x1, Pallas kernels, body(): pl.pallas_call(weighted_sum, out_shape=jax.ShapeDtypeStruct((tokens, widt...  1.82 us

profile of v4, /device:TPU:0, one launch (start us, length us, event | category | flops | bytes accessed | tf_op | source)
XLA Modules:
  0.0 41.9 jit_solution(9332437122711116039)
XLA Ops:
  0.0 40.1 %expert_layer.1 = (bf16[4,2,6144]{2,1,0:T(2,128)(2,1)}, f32[8,4]{1,0:T(8,128)}) custom-call(bf16[4,6144]{1,0:T(4,128)(2,1)} %hid_hbm.1, f32[1,6144]{1,0:T(1,128)} %bitcast.3, s32[2,4]{1,0:T(2,128)} %bitcast.4, f32[2,4]{1,0:T(2,128)} %bitcast.5, bf16[1,6144,1024]{2,1,0:T(8,128)(2,1)} %wg.1, bf16[1,6144,1024]{2,1,0:T(8,128)(2,1)} %wu.1, bf16[1,1024,6144]{2,1,0:T(8,128)(2,1)} %wd.1), custom_call_target="tpu_custom_call" | custom-call | flops 2415919104 | bytes 37748736 | tf_op jit(solution)/shard_map/expert_layer/pallas_call | solution.py:249
  40.1 1.8 %weighted_sum.1 = bf16[4,6144]{1,0:T(4,128)(2,1)} custom-call(bf16[4,2,6144]{2,1,0:T(2,128)(2,1)} %get-tuple-element.7.back_hbm, f32[8,4]{1,0:T(8,128)} %get-tuple-element.8.coef_hbm), custom_call_target="tpu_custom_call" | custom-call | tf_op jit(solution)/shard_map/weighted_sum/pallas_call | solution.py:302

commit v5 on v4

--- a/solution.py
+++ b/solution.py
@@ -79,10 +79,7 @@
         for copy in wcopies[c]:
             copy.start()
 
-    for c in range(kchunks):
-        fetch(c)
-    for copy in dcopies:
-        copy.start()
+    fetch(0)
     for copy in small:
         copy.wait()
 
@@ -121,6 +118,8 @@
     for c in range(kchunks):
         for k, e in enumerate(z_peers):
             go(remote(zsend.at[c, e], zrecv.at[c, me_e], zss.at[c, k], zrs.at[c, me_e], z_dev(e)))
+    for c in range(1, kchunks):
+        fetch(c)
     for c in range(kchunks):
         zrecv[c, me_e] = zsend[c, me_e]
 
@@ -162,7 +161,10 @@
 
     for c in range(kchunks):
         spread(c)
+    dcopies[0].start()
     forward(0)
+    for copy in dcopies[1:]:
+        copy.start()
     for c in range(kchunks):
         if c + 1 < kchunks:
             forward(c + 1)
@@ -239,7 +241,7 @@
     experts, tps, dps = lax.axis_size("expert"), lax.axis_size("tp"), lax.axis_size("dp")
     tokens, width = hidden.shape
     inner = w_gate.shape[2]
-    kchunks, ochunks = 3, 6
+    kchunks, ochunks = 2, 3
     kc, oc = width // kchunks, width // ochunks
     group = tps * (dps // 2)
     rows = experts * MOST

time: 42 us -> 34.3 us (0.82)
  Pallas kernels: 41.9 us -> 34.2 us
    pallas_call x1, Pallas kernels: 40.1 us -> 32.3 us  [body(): pl.pallas_call(functools.partial(kernel, experts, tps, dps, kchunks, ochu...]
where the time goes in v5:
time: 34.3 us; the launch traced here: 34.2 us
  Pallas kernels  34.2 us (100%)
    pallas_call x1, Pallas kernels, body(): pl.pallas_call(functools.partial(kernel, experts, tps, dps, kchunks, ochu...  32.3 us
    pallas_call x1, Pallas kernels, body(): pl.pallas_call(weighted_sum, out_shape=jax.ShapeDtypeStruct((tokens, widt...  1.82 us

profile of v5, /device:TPU:0, one launch (start us, length us, event | category | flops | bytes accessed | tf_op | source)
XLA Modules:
  0.0 34.2 jit_solution(9726008971052618542)
XLA Ops:
  0.0 32.3 %expert_layer.1 = (bf16[4,2,6144]{2,1,0:T(2,128)(2,1)}, f32[8,4]{1,0:T(8,128)}) custom-call(bf16[4,6144]{1,0:T(4,128)(2,1)} %hid_hbm.1, f32[1,6144]{1,0:T(1,128)} %bitcast.3, s32[2,4]{1,0:T(2,128)} %bitcast.4, f32[2,4]{1,0:T(2,128)} %bitcast.5, bf16[1,6144,1024]{2,1,0:T(8,128)(2,1)} %wg.1, bf16[1,6144,1024]{2,1,0:T(8,128)(2,1)} %wu.1, bf16[1,1024,6144]{2,1,0:T(8,128)(2,1)} %wd.1), custom_call_target="tpu_custom_call" | custom-call | flops 2415919104 | bytes 37748736 | tf_op jit(solution)/shard_map/expert_layer/pallas_call | solution.py:251
  32.3 1.8 %weighted_sum.1 = bf16[4,6144]{1,0:T(4,128)(2,1)} custom-call(bf16[4,2,6144]{2,1,0:T(2,128)(2,1)} %get-tuple-element.7.back_hbm, f32[8,4]{1,0:T(8,128)} %get-tuple-element.8.coef_hbm), custom_call_target="tpu_custom_call" | custom-call | tf_op jit(solution)/shard_map/weighted_sum/pallas_call | solution.py:304
